TPU v7x, 32 devices: a whole 2x2x4 slice. The times are simulated.
32 devices in a mesh: loop: 2 (over core), dp: 16 (over z, y, x).
Axes of the slice: x: 2, y: 2, z: 4, core: 2. Of those that a mesh axis runs over, the one named last changes fastest.
Arguments:
- tokens: bfloat16 [4096, 4096], P('dp', 'loop'), may hold values from -6 to 6
- probs: float32 [4096, 2], P('dp'), may hold values from 0.05 to 1
- routes: int32 [4096, 2], P('dp'), may hold values from 0 to 15, all different within a row; in each aligned block of 256 rows (0 to 255, 256 to 511, ...) at most 48 rows name the same one
- out_grad: bfloat16 [4096, 4096], P('dp', 'loop'), may hold values from -6 to 6
- w_gate: bfloat16 [16, 1536, 4096], P('dp', 'loop'), may hold values from -0.09375 to 0.09375
- w_up: bfloat16 [16, 1536, 4096], P('dp', 'loop'), may hold values from -0.09375 to 0.09375
- w_down: bfloat16 [16, 1536, 4096], P('dp', 'loop'), may hold values from -0.15625 to 0.15625
Outputs:
- layer_out: bfloat16 [4096, 4096], P('dp', 'loop')
- input_grad: bfloat16 [4096, 4096], P('dp', 'loop')
- prob_grad: float32 [4096, 2], P('dp')
- grad_gate: bfloat16 [16, 1536, 4096], P('dp', 'loop')
- grad_up: bfloat16 [16, 1536, 4096], P('dp', 'loop')
- grad_down: bfloat16 [16, 1536, 4096], P('dp', 'loop')
Inputs may be any that keep to these rules, and one draw needn't show every extreme that they name: `routes`: A token's 2 experts differ. Among the 256 tokens of one dp index no expert is named more than 48 times, and in every draw some expert is named exactly 48 times there.
All inputs are finite; a program needn't handle non-finite values.
Results may differ from a plain program's by a relative error of at most 0.0072.
Values may be sent and summed in bfloat16 or wider, within the bound.
A program may use at most 192 MiB of HBM per device.

v0:
```python
import jax
import jax.numpy as jnp
from jax import lax
from jax.sharding import PartitionSpec as P


def shards(tokens, probs, routes, out_grad, w_gate, w_up, w_down):
    tok_count = tokens.shape[0]
    top_count = routes.shape[1]
    experts = lax.axis_size("dp")
    capacity = max(2, 3 * tok_count * top_count // (2 * experts))
    flat = routes.reshape(-1)
    labels = jnp.arange(experts, dtype=jnp.int32)
    onehot = (flat[:, None] == labels[None, :]).astype(jnp.int32)
    before = jnp.cumsum(onehot, axis=0) - onehot
    target = flat * capacity + jnp.sum(before * onehot, axis=1)

    def spread(values):
        width = values.shape[-1]
        buffer = jnp.zeros((experts * capacity, width), values.dtype)
        buffer = buffer.at[target].set(values.reshape(-1, width))
        return buffer.reshape(experts, capacity, width)

    whole_x, whole_g = (
        lax.all_gather(tokens, "loop", axis=1, tiled=True),
        lax.all_gather(out_grad, "loop", axis=1, tiled=True),
    )
    scaled = (probs[:, :, None] * whole_g[:, None, :].astype(jnp.float32)).astype(jnp.bfloat16)
    copies = jnp.broadcast_to(whole_x[:, None, :], (tok_count, top_count, whole_x.shape[1]))
    recv_x, recv_g = (
        lax.all_to_all(spread(copies), "dp", split_axis=0, concat_axis=0, tiled=True),
        lax.all_to_all(spread(scaled), "dp", split_axis=0, concat_axis=0, tiled=True),
    )
    width_full = recv_x.shape[-1]
    rows_x = recv_x.reshape(-1, width_full)
    rows_g = recv_g.reshape(-1, width_full)
    gate_rows = w_gate[0]
    up_rows = w_up[0]
    down_rows = w_down[0]
    contract = (((1,), (1,)), ((), ()))
    gate = lax.dot_general(rows_x, gate_rows, contract, preferred_element_type=jnp.float32)
    up = lax.dot_general(rows_x, up_rows, contract, preferred_element_type=jnp.float32)
    sig = jax.nn.sigmoid(gate)
    silu = gate * sig
    hidden = (silu * up).astype(jnp.bfloat16)
    out_part = jnp.dot(hidden, down_rows, preferred_element_type=jnp.float32)
    dhid = lax.dot_general(rows_g, down_rows, contract, preferred_element_type=jnp.float32)
    dgate = (dhid * up * sig * (1.0 + gate * (1.0 - sig))).astype(jnp.bfloat16)
    dup = (dhid * silu).astype(jnp.bfloat16)
    dx_part = jnp.dot(dgate, gate_rows, preferred_element_type=jnp.float32) + jnp.dot(
        dup, up_rows, preferred_element_type=jnp.float32
    )
    outer = (((0,), (0,)), ((), ()))
    grad_gate = lax.dot_general(dgate, rows_x, outer, preferred_element_type=jnp.float32).astype(
        jnp.bfloat16
    )[None]
    grad_up = lax.dot_general(dup, rows_x, outer, preferred_element_type=jnp.float32).astype(
        jnp.bfloat16
    )[None]
    grad_down = lax.dot_general(hidden, rows_g, outer, preferred_element_type=jnp.float32).astype(
        jnp.bfloat16
    )[None]
    out_sum, dx_sum = (
        lax.psum_scatter(
            out_part.astype(jnp.bfloat16), "loop", scatter_dimension=1, tiled=True
        ).astype(jnp.float32),
        lax.psum_scatter(
            dx_part.astype(jnp.bfloat16), "loop", scatter_dimension=1, tiled=True
        ).astype(jnp.float32),
    )
    width_part = out_sum.shape[1]
    back_out, back_dx = (
        lax.all_to_all(
            out_sum.astype(jnp.bfloat16).reshape(experts, capacity, width_part),
            "dp",
            split_axis=0,
            concat_axis=0,
            tiled=True,
        ),
        lax.all_to_all(
            dx_sum.astype(jnp.bfloat16).reshape(experts, capacity, width_part),
            "dp",
            split_axis=0,
            concat_axis=0,
            tiled=True,
        ),
    )
    out_rows = (
        back_out.reshape(experts * capacity, width_part)[target]
        .reshape(tok_count, top_count, width_part)
        .astype(jnp.float32)
    )
    dx_rows = (
        back_dx.reshape(experts * capacity, width_part)[target]
        .reshape(tok_count, top_count, width_part)
        .astype(jnp.float32)
    )
    layer_out = jnp.sum(probs[:, :, None] * out_rows, axis=1).astype(jnp.bfloat16)
    input_grad = jnp.sum(dx_rows, axis=1).astype(jnp.bfloat16)
    partial_dots = jnp.sum(out_grad.astype(jnp.float32)[:, None, :] * out_rows, axis=2)
    prob_grad = lax.psum(partial_dots, "loop")
    return (layer_out, input_grad, prob_grad, grad_gate, grad_up, grad_down)


def solution(mesh):
    in_specs = (
        P("dp", "loop"),
        P("dp", None),
        P("dp", None),
        P("dp", "loop"),
        P("dp", "loop", None),
        P("dp", "loop", None),
        P("dp", "loop", None),
    )
    out_specs = (
        P("dp", "loop"),
        P("dp", "loop"),
        P("dp", None),
        P("dp", "loop", None),
        P("dp", "loop", None),
        P("dp", "loop", None),
    )
    return jax.shard_map(shards, mesh=mesh, in_specs=in_specs, out_specs=out_specs, check_vma=False)
```

profile of v0, /device:TPU:12, one launch (start us, length us, event | category | flops | bytes accessed | tf_op | source)
XLA Modules:
  0.0 571.3 jit_solution(12507158925894243836)
XLA Ops:
  11.5 10.0 %all-gather.3.cloned.1.call-done = bf16[256,4096]{1,0:T(8,128)(2,1)} async-done(((bf16[256,2048]{1,0:T(8,128)(2,1)}), bf16[256,4096]{1,0:T(8,128)(2,1)}) %all-gather.3.cloned.1.call-update) | async-done | bytes 2097168 | tf_op jit(solution)/shard_map/all_gather | solution.py:25
  21.6 6.0 %broadcast_in_dim.8 = bf16[256,2,4096]{2,1,0:T(2,128)(2,1)} broadcast(bf16[256,4096]{1,0:T(8,128)(2,1)} %all-gather.3.cloned.1.call-done), dimensions={0,2} | broadcast | bytes 6291456 | tf_op jit(solution)/shard_map/broadcast_in_dim | solution.py:29
  27.6 7.2 %reshape.141 = bf16[512,4096]{1,0:T(8,128)(2,1)} reshape(bf16[256,2,4096]{2,1,0:T(2,128)(2,1)} %broadcast_in_dim.8) | data formatting | bytes 8388608 | tf_op jit(solution)/shard_map/reshape | solution.py:21
  34.7 11.4 %scatter_custom_fusion = bf16[768,4096]{1,0:T(8,128)(2,1)} fusion(s32[512]{0:T(512)S(1)} %bitcast.69, bf16[512,4096]{1,0:T(8,128)(2,1)} %reshape.141, bf16[]{:T(256)} %constant.6.clone.1), kind=kCustom, calls=%fused_computation.28 | custom fusion | bytes 6291968 | tf_op jit(solution)/shard_map/scatter | solution.py:21
  46.2 7.1 %all-to-all-start = ((bf16[16,48,4096]{2,1,0:T(8,128)(2,1)}), bf16[16,48,4096]{2,1,0:T(8,128)(2,1)}, u32[]{:S(2)}, u32[]{:S(2)}) async-start(bf16[16,48,4096]{2,1,0:T(8,128)(2,1)} %bitcast.65), calls=%async_computation | async-start | bytes 12582912 | tf_op jit(solution)/shard_map/all_to_all | solution.py:31
  54.3 13.1 %all-gather.5.cloned.1.call-done = bf16[256,4096]{1,0:T(8,128)(2,1)} async-done(((bf16[256,2048]{1,0:T(8,128)(2,1)}), bf16[256,4096]{1,0:T(8,128)(2,1)}) %all-gather.5.cloned.1.call-update) | async-done | bytes 2097168 | tf_op jit(solution)/shard_map/all_gather | solution.py:26
  67.4 8.3 %mul.88 = f32[256,2,4096]{2,1,0:T(2,128)} broadcast(bf16[256,4096]{1,0:T(8,128)(2,1)} %all-gather.5.cloned.1.call-done), dimensions={0,2} | broadcast | bytes 10485760 | tf_op jit(solution)/shard_map/mul | solution.py:28
  75.7 10.9 %mul.89 = f32[512,4096]{1,0:T(8,128)} reshape(f32[256,2,4096]{2,1,0:T(2,128)} %mul.88) | data formatting | bytes 16777216 | tf_op jit(solution)/shard_map/mul | solution.py:28
  86.6 12.7 %scatter_custom_fusion.1 = bf16[768,4096]{1,0:T(8,128)(2,1)} fusion(s32[512]{0:T(512)S(1)} %bitcast.70, f32[512,4096]{1,0:T(8,128)} %mul.89, f32[512]{0:T(512)S(1)} %mul.86, bf16[]{:T(256)} %constant.6.clone.1), kind=kCustom, calls=%fused_computation.23 | custom fusion | flops 4194304 | bytes 14682114 | tf_op jit(solution)/shard_map/scatter | solution.py:21
  99.3 96.2 %all-to-all-done = bf16[16,48,4096]{2,1,0:T(8,128)(2,1)} async-done(((bf16[16,48,4096]{2,1,0:T(8,128)(2,1)}), bf16[16,48,4096]{2,1,0:T(8,128)(2,1)}, u32[]{:S(2)}, u32[]{:S(2)}) %all-to-all-start) | async-done | bytes 6291488 | tf_op jit(solution)/shard_map/all_to_all | solution.py:31
  195.5 7.4 %all-to-all-start.2 = ((bf16[16,48,4096]{2,1,0:T(8,128)(2,1)}), bf16[16,48,4096]{2,1,0:T(8,128)(2,1)}, u32[]{:S(2)}, u32[]{:S(2)}) async-start(bf16[16,48,4096]{2,1,0:T(8,128)(2,1)} %bitcast.66), calls=%async_computation.3 | async-start | bytes 12582912 | tf_op jit(solution)/shard_map/all_to_all | solution.py:32
  203.1 10.2 %fusion.4 = f32[768,768]{1,0:T(8,128)} fusion(bf16[768,4096]{1,0:T(8,128)(2,1)} %bitcast.4, bf16[1,768,4096]{2,1,0:T(8,128)(2,1)} %param.12), kind=kOutput, calls=%fused_computation.14 | convolution fusion | flops 4831838208 | bytes 14942208 | tf_op jit(solution)/shard_map/dot_general | solution.py:42
  213.3 8.2 %fusion.8 = f32[768,768]{1,0:T(8,128)} fusion(bf16[768,4096]{1,0:T(8,128)(2,1)} %bitcast.4, bf16[1,768,4096]{2,1,0:T(8,128)(2,1)S(1)} %bitcast.74), kind=kOutput, calls=%fused_computation.18 | convolution fusion | flops 4831838208 | bytes 14942208 | tf_op jit(solution)/shard_map/dot_general | solution.py:41
  221.5 120.8 %all-to-all-done.2 = bf16[16,48,4096]{2,1,0:T(8,128)(2,1)} async-done(((bf16[16,48,4096]{2,1,0:T(8,128)(2,1)}), bf16[16,48,4096]{2,1,0:T(8,128)(2,1)}, u32[]{:S(2)}, u32[]{:S(2)}) %all-to-all-start.2) | async-done | bytes 6291488 | tf_op jit(solution)/shard_map/all_to_all | solution.py:32
  342.3 11.8 %multiply_convert_fusion.2 = (bf16[768,768]{1,0:T(8,128)(2,1)S(1)}, bf16[768,768]{1,0:T(8,128)(2,1)}, bf16[768,768]{1,0:T(8,128)(2,1)S(1)}) fusion(f32[768,768]{1,0:T(8,128)} %fusion.8, f32[768,768]{1,0:T(8,128)} %fusion.4, bf16[768,4096]{1,0:T(8,128)(2,1)} %bitcast.11, bf16[1,768,4096]{2,1,0:T(8,128)(2,1)} %param.13), kind=kOutput, calls=%fused_computation.30 | convolution fusion | flops 4840685568 | bytes 20840448 | tf_op jit(solution)/shard_map/dot_general | solution.py:47
  354.1 8.4 %fusion.6 = f32[768,4096]{1,0:T(8,128)S(1)} fusion(bf16[768,768]{1,0:T(8,128)(2,1)} %get-tuple-element.15, bf16[1,768,4096]{2,1,0:T(8,128)(2,1)} %param.11), kind=kOutput, calls=%fused_computation.16 | convolution fusion | flops 4831838208 | bytes 20054016 | tf_op jit(solution)/shard_map/dot_general | solution.py:50
  362.5 6.9 %add_convert_fusion = bf16[768,4096]{1,0:T(8,128)(2,1)} fusion(f32[768,4096]{1,0:T(8,128)S(1)} %fusion.6, bf16[768,768]{1,0:T(8,128)(2,1)S(1)} %get-tuple-element.14, bf16[1,768,4096]{2,1,0:T(8,128)(2,1)S(1)} %bitcast.76), kind=kOutput, calls=%fused_computation.4 | convolution fusion | flops 4838129664 | bytes 26345472 | tf_op jit(solution)/shard_map/dot_general | solution.py:50
  369.7 10.2 %convolution_convert_fusion.3 = bf16[768,4096]{1,0:T(8,128)(2,1)} fusion(bf16[768,768]{1,0:T(8,128)(2,1)S(1)} %get-tuple-element.16, bf16[1,768,4096]{2,1,0:T(8,128)(2,1)} %param.13), kind=kOutput, calls=%fused_computation.9 | convolution fusion | flops 4834983936 | bytes 13762560 | tf_op jit(solution)/shard_map/dot_general | solution.py:46
  379.9 4.2 reduce-scatter.5.cloned.1.call-done
  384.1 7.0 %all-to-all-start.3 = ((bf16[16,48,2048]{2,1,0:T(8,128)(2,1)}), bf16[16,48,2048]{2,1,0:T(8,128)(2,1)S(1)}, u32[]{:S(2)}, u32[]{:S(2)}) async-start(bf16[16,48,2048]{2,1,0:T(8,128)(2,1)} %bitcast.68), calls=%async_computation.5 | async-start | bytes 6291456 | tf_op jit(solution)/shard_map/all_to_all | solution.py:80
  391.1 11.6 %reduce-scatter.3.cloned.1.call-done = bf16[768,2048]{1,0:T(8,128)(2,1)} async-done(((bf16[768,4096]{1,0:T(8,128)(2,1)}), bf16[768,2048]{1,0:T(8,128)(2,1)}) %reduce-scatter.3.cloned.1.call-update) | async-done | bytes 3145744 | tf_op jit(solution)/shard_map/reduce_scatter | solution.py:64
  402.7 60.0 %all-to-all-done.3 = bf16[16,48,2048]{2,1,0:T(8,128)(2,1)S(1)} async-done(((bf16[16,48,2048]{2,1,0:T(8,128)(2,1)}), bf16[16,48,2048]{2,1,0:T(8,128)(2,1)S(1)}, u32[]{:S(2)}, u32[]{:S(2)}) %all-to-all-start.3) | async-done | bytes 3145760 | tf_op jit(solution)/shard_map/all_to_all | solution.py:80
  462.6 6.0 %all-to-all-start.1 = ((bf16[16,48,2048]{2,1,0:T(8,128)(2,1)}), bf16[16,48,2048]{2,1,0:T(8,128)(2,1)}, u32[]{:S(2)}, u32[]{:S(2)}) async-start(bf16[16,48,2048]{2,1,0:T(8,128)(2,1)} %bitcast.67), calls=%async_computation.2 | async-start | bytes 6291456 | tf_op jit(solution)/shard_map/all_to_all | solution.py:73
  471.4 9.3 %fusion.10 = bf16[1,768,4096]{2,1,0:T(8,128)(2,1)} fusion(bf16[768,768]{1,0:T(8,128)(2,1)} %get-tuple-element.15, bf16[768,4096]{1,0:T(8,128)(2,1)} %bitcast.4), kind=kOutput, calls=%fused_computation.20 | convolution fusion | flops 4834983936 | bytes 13762560 | tf_op jit(solution)/shard_map/dot_general | solution.py:54
  480.7 9.9 %fusion.11 = bf16[1,768,4096]{2,1,0:T(8,128)(2,1)} fusion(bf16[768,768]{1,0:T(8,128)(2,1)S(1)} %copy-done.2, bf16[768,4096]{1,0:T(8,128)(2,1)} %bitcast.4), kind=kOutput, calls=%fused_computation.21 | convolution fusion | flops 4834983936 | bytes 13762560 | tf_op jit(solution)/shard_map/dot_general | solution.py:57
  490.6 9.8 %fusion.12 = bf16[1,768,4096]{2,1,0:T(8,128)(2,1)} fusion(bf16[768,768]{1,0:T(8,128)(2,1)S(1)} %copy-done.4, bf16[768,4096]{1,0:T(8,128)(2,1)} %bitcast.11), kind=kOutput, calls=%fused_computation.22 | convolution fusion | flops 4834983936 | bytes 13762560 | tf_op jit(solution)/shard_map/dot_general | solution.py:60
  507.2 6.7 %reduce_sum.44 = bf16[256,2048]{1,0:T(8,128)(2,1)} reduce(bf16[256,2,2048]{2,1,0:T(2,128)(2,1)S(1)} %reshape.119, bf16[]{:T(256)} %constant.6.clone.1), dimensions={1}, to_apply=%region_8.9 | reduce | flops 524288 | bytes 3145730 | tf_op jit(solution)/shard_map/reduce_sum | solution.py:99
  513.9 24.8 %all-to-all-done.1 = bf16[16,48,2048]{2,1,0:T(8,128)(2,1)} async-done(((bf16[16,48,2048]{2,1,0:T(8,128)(2,1)}), bf16[16,48,2048]{2,1,0:T(8,128)(2,1)}, u32[]{:S(2)}, u32[]{:S(2)}) %all-to-all-start.1) | async-done | bytes 3145760 | tf_op jit(solution)/shard_map/all_to_all | solution.py:73
  538.7 6.7 %gather_fusion = bf16[512,2048]{1,0:T(8,128)(2,1)S(1)} fusion(bf16[768,2048]{1,0:T(8,128)(2,1)} %bitcast.9, s32[1024]{0:T(1024)S(1)} %pad_clamp_fusion), kind=kCustom, calls=%fused_computation | custom fusion | bytes 4196352 | tf_op jit(solution)/shard_map/gather | solution.py:89
  545.4 4.0 reshape.120
  549.3 10.6 %multiply_reduce_fusion = (f32[256,2]{1,0:T(8,128)S(1)}, bf16[256,2048]{1,0:T(8,128)(2,1)}) fusion(f32[256,2,2048]{2,1,0:T(2,128)} %reshape.120, f32[256,2048]{1,0:T(8,128)} %convert_element_type.73, f32[256,2]{1,0:T(8,128)S(1)} %copy.20), kind=kLoop, calls=%fused_computation.24 | loop fusion | flops 3669504 | bytes 7344128 | tf_op jit(solution)/shard_map/reduce_sum | solution.py:100
  559.9 3.7 psum.7
  (48 shorter events, 16.0 us)
Async XLA Ops:
  7.2 14.4 %all-gather.3.cloned.1.call-start = ((), (), s32[]{:S(2)}) async-start(), calls=%async_computation.6 | async-start | bytes 3145728 | tf_op jit(solution)/shard_map/all_gather | solution.py:25
  46.2 7.8 %copy-start = (f32[256,2]{0,1:T(2,128)S(1)}, f32[256,2]{0,1:T(2,128)}, u32[]{:S(2)}) copy-start(f32[256,2]{0,1:T(2,128)} %param.8) | copy-start | bytes 6148
  46.2 149.3 %all-to-all-start = ((bf16[16,48,4096]{2,1,0:T(8,128)(2,1)}), bf16[16,48,4096]{2,1,0:T(8,128)(2,1)}, u32[]{:S(2)}, u32[]{:S(2)}) async-start(bf16[16,48,4096]{2,1,0:T(8,128)(2,1)} %bitcast.65), calls=%async_computation | async-start | bytes 12582912 | tf_op jit(solution)/shard_map/all_to_all | solution.py:31
  53.3 14.1 %all-gather.5.cloned.1.call-start = ((), (), s32[]{:S(2)}) async-start(), calls=%async_computation.8 | async-start | bytes 3145728 | tf_op jit(solution)/shard_map/all_gather | solution.py:26
  195.5 17.8 %slice-start = ((s8[6291456]{0:T(1024)(128)(4,1)}), s8[2097152]{0:T(1024)(128)(4,1)S(1)}, s32[]{:S(2)}) async-start(s8[6291456]{0:T(1024)(128)(4,1)} %bitcast.73), calls=%async_computation.10 | async-start | bytes 4194304
  195.5 146.8 %all-to-all-start.2 = ((bf16[16,48,4096]{2,1,0:T(8,128)(2,1)}), bf16[16,48,4096]{2,1,0:T(8,128)(2,1)}, u32[]{:S(2)}, u32[]{:S(2)}) async-start(bf16[16,48,4096]{2,1,0:T(8,128)(2,1)} %bitcast.66), calls=%async_computation.3 | async-start | bytes 12582912 | tf_op jit(solution)/shard_map/all_to_all | solution.py:32
  202.8 181.3 %reduce-scatter.5.cloned.1.call-start = ((), (), s32[]{:S(2)}) async-start(), calls=%async_computation.9 | async-start | bytes 9437184 | tf_op jit(solution)/shard_map/reduce_scatter | solution.py:67
  203.0 10.2 %slice-start.1 = ((s8[6291456]{0:T(1024)(128)(4,1)}), s8[4194304]{0:T(1024)(128)(4,1)S(1)}, s32[]{:S(2)}) async-start(s8[6291456]{0:T(1024)(128)(4,1)} %bitcast.73), calls=%async_computation.11 | async-start | bytes 8388608
  342.3 20.1 %slice-start.2 = ((s8[6291456]{0:T(1024)(128)(4,1)}), s8[2097152]{0:T(1024)(128)(4,1)S(1)}, s32[]{:S(2)}) async-start(s8[6291456]{0:T(1024)(128)(4,1)} %bitcast.75), calls=%async_computation.12 | async-start | bytes 4194304
  354.1 8.4 %copy-start.1 = (bf16[768,768]{1,0:T(8,128)(2,1)}, bf16[768,768]{1,0:T(8,128)(2,1)S(1)}, u32[]{:S(2)}) copy-start(bf16[768,768]{1,0:T(8,128)(2,1)S(1)} %get-tuple-element.14) | copy-start | bytes 3538948
  354.1 15.6 %copy-start.3 = (bf16[768,768]{1,0:T(8,128)(2,1)}, bf16[768,768]{1,0:T(8,128)(2,1)S(1)}, u32[]{:S(2)}) copy-start(bf16[768,768]{1,0:T(8,128)(2,1)S(1)} %get-tuple-element.16) | copy-start | bytes 3538948
  354.1 8.4 %slice-start.3 = ((s8[6291456]{0:T(1024)(128)(4,1)}), s8[4194304]{0:T(1024)(128)(4,1)S(1)}, s32[]{:S(2)}) async-start(s8[6291456]{0:T(1024)(128)(4,1)} %bitcast.75), calls=%async_computation.13 | async-start | bytes 8388608
  369.4 33.3 %reduce-scatter.3.cloned.1.call-start = ((), (), s32[]{:S(2)}) async-start(), calls=%async_computation.7 | async-start | bytes 9437184 | tf_op jit(solution)/shard_map/reduce_scatter | solution.py:64
  384.1 78.5 %all-to-all-start.3 = ((bf16[16,48,2048]{2,1,0:T(8,128)(2,1)}), bf16[16,48,2048]{2,1,0:T(8,128)(2,1)S(1)}, u32[]{:S(2)}, u32[]{:S(2)}) async-start(bf16[16,48,2048]{2,1,0:T(8,128)(2,1)} %bitcast.68), calls=%async_computation.5 | async-start | bytes 6291456 | tf_op jit(solution)/shard_map/all_to_all | solution.py:80
  462.6 76.0 %all-to-all-start.1 = ((bf16[16,48,2048]{2,1,0:T(8,128)(2,1)}), bf16[16,48,2048]{2,1,0:T(8,128)(2,1)}, u32[]{:S(2)}, u32[]{:S(2)}) async-start(bf16[16,48,2048]{2,1,0:T(8,128)(2,1)} %bitcast.67), calls=%async_computation.2 | async-start | bytes 6291456 | tf_op jit(solution)/shard_map/all_to_all | solution.py:73
  471.4 9.3 %copy-start.2 = (bf16[768,768]{1,0:T(8,128)(2,1)S(1)}, bf16[768,768]{1,0:T(8,128)(2,1)}, u32[]{:S(2)}) copy-start(bf16[768,768]{1,0:T(8,128)(2,1)} %copy-done.1) | copy-start | bytes 3538948
  480.7 9.9 %copy-start.4 = (bf16[768,768]{1,0:T(8,128)(2,1)S(1)}, bf16[768,768]{1,0:T(8,128)(2,1)}, u32[]{:S(2)}) copy-start(bf16[768,768]{1,0:T(8,128)(2,1)} %copy-done.3) | copy-start | bytes 3538948
Sparse Core Ops, SparseCore 0:
  9.5 11.9 all-gather.2
  55.7 11.6 all-gather.4
  369.5 14.5 reduce-scatter.4
  386.9 15.6 reduce-scatter.2
where the time goes:
time: 581 us; the launch traced here: 571 us
  waiting for transfers between devices  342 us (59%)
  matrix products  84.6 us (15%)
  local copies, waits for them, and re-layouts  63.8 us (11%)
  other arithmetic  34.8 us (6%)
  starting transfers between devices  28.4 us (5%)
  between operations  14.4 us (2%)
    all_to_all x1, waiting for transfers between devices, shards(): lax.all_to_all(spread(scaled), 'dp', split_axis=0, concat_axis=0, tiled=T...  121 us
    all_to_all x1, waiting for transfers between devices, shards(): lax.all_to_all(spread(copies), 'dp', split_axis=0, concat_axis=0, tiled=T...  96.2 us
    all_to_all x1, waiting for transfers between devices, shards(): lax.all_to_all(dx_sum.astype(jnp.bfloat16).reshape(experts, capacity, wid...  60 us
    all_to_all x1, waiting for transfers between devices, shards(): lax.all_to_all(out_sum.astype(jnp.bfloat16).reshape(experts, capacity, wi...  24.8 us
    mul x3, local copies, waits for them, and re-layouts, shards(): probs[:, :, None] * whole_g[:, None, :].astype(jnp.float32)  19.3 us
    all_gather x1, waiting for transfers between devices, shards(): lax.all_gather(out_grad, 'loop', axis=1, tiled=True)  13.1 us
    scatter x1, other arithmetic, spread(): buffer = buffer.at[target].set(values.reshape(-1, width))  12.7 us
    dot_general x1, matrix products, shards(): lax.dot_general(rows_g, down_rows, contract, preferred_element_type=jnp.f...  11.8 us
  transfers between devices with their start and end apart: 8, of which 8 were waited for; matrix products, arithmetic and copies ran while one was open for 19% of the time, Pallas kernels for 0%

commit v1 on v0

v1 whole, which is shorter than its diff:
```python
import jax
import jax.numpy as jnp
from jax import lax
from jax.sharding import PartitionSpec as P


def shards(tokens, probs, routes, out_grad, w_gate, w_up, w_down):
    tok_count = tokens.shape[0]
    top_count = routes.shape[1]
    experts = lax.axis_size("dp")
    capacity = max(2, 3 * tok_count * top_count // (2 * experts))
    flat = routes.reshape(-1)
    count = flat.shape[0]
    labels = jnp.arange(experts, dtype=jnp.int32)
    onehot = flat[:, None] == labels[None, :]
    place = jnp.arange(count, dtype=jnp.int32)
    earlier = (place[None, :] < place[:, None]).astype(jnp.bfloat16)
    before = jnp.dot(earlier, onehot.astype(jnp.bfloat16), preferred_element_type=jnp.float32)
    rank = jnp.sum(jnp.where(onehot, before, 0.0), axis=1).astype(jnp.int32)
    target = (flat * capacity + rank).reshape(tok_count, top_count)
    slots = jnp.arange(experts * capacity, dtype=jnp.int32)
    picks = [slots[:, None] == target[:, k][None, :] for k in range(top_count)]
    pick = sum(p.astype(jnp.bfloat16) for p in picks)
    slot_prob = sum(
        jnp.sum(jnp.where(picks[k], probs[:, k][None, :], 0.0), axis=1) for k in range(top_count)
    )
    send_x = jnp.dot(pick, tokens, preferred_element_type=jnp.float32).astype(jnp.bfloat16)
    send_g = (
        jnp.dot(pick, out_grad, preferred_element_type=jnp.float32) * slot_prob[:, None]
    ).astype(jnp.bfloat16)

    def exchange(rows):
        cut = rows.reshape(experts, capacity, rows.shape[-1])
        moved = lax.all_to_all(cut, "dp", split_axis=0, concat_axis=0, tiled=True)
        return moved.reshape(experts * capacity, rows.shape[-1])

    part_x = exchange(send_x)
    part_x, send_g = lax.optimization_barrier((part_x, send_g))
    part_g = exchange(send_g)
    rows_x = lax.all_gather(part_x, "loop", axis=1, tiled=True)
    rows_g = lax.all_gather(part_g, "loop", axis=1, tiled=True)
    gate_rows = w_gate[0]
    up_rows = w_up[0]
    down_rows = w_down[0]
    contract = (((1,), (1,)), ((), ()))
    gate = lax.dot_general(rows_x, gate_rows, contract, preferred_element_type=jnp.float32)
    up = lax.dot_general(rows_x, up_rows, contract, preferred_element_type=jnp.float32)
    sig = jax.nn.sigmoid(gate)
    silu = gate * sig
    hidden = (silu * up).astype(jnp.bfloat16)
    out_part = jnp.dot(hidden, down_rows, preferred_element_type=jnp.float32)
    dhid = lax.dot_general(rows_g, down_rows, contract, preferred_element_type=jnp.float32)
    dgate = (dhid * up * sig * (1.0 + gate * (1.0 - sig))).astype(jnp.bfloat16)
    dup = (dhid * silu).astype(jnp.bfloat16)
    dx_part = jnp.dot(dgate, gate_rows, preferred_element_type=jnp.float32) + jnp.dot(
        dup, up_rows, preferred_element_type=jnp.float32
    )
    outer = (((0,), (0,)), ((), ()))
    grad_gate = lax.dot_general(dgate, rows_x, outer, preferred_element_type=jnp.float32).astype(
        jnp.bfloat16
    )[None]
    grad_up = lax.dot_general(dup, rows_x, outer, preferred_element_type=jnp.float32).astype(
        jnp.bfloat16
    )[None]
    grad_down = lax.dot_general(hidden, rows_g, outer, preferred_element_type=jnp.float32).astype(
        jnp.bfloat16
    )[None]
    out_sum = lax.psum_scatter(
        out_part.astype(jnp.bfloat16), "loop", scatter_dimension=1, tiled=True
    )
    back_out = exchange(out_sum)
    dx_sum = lax.psum_scatter(
        dx_part.astype(jnp.bfloat16), "loop", scatter_dimension=1, tiled=True
    )
    back_out, dx_sum = lax.optimization_barrier((back_out, dx_sum))
    back_dx = exchange(dx_sum)
    wanted = [(target[:, k][:, None] == slots[None, :]) for k in range(top_count)]
    out_rows = [
        jnp.dot(w.astype(jnp.bfloat16), back_out, preferred_element_type=jnp.float32)
        for w in wanted
    ]
    layer_out = sum(probs[:, k][:, None] * out_rows[k] for k in range(top_count)).astype(
        jnp.bfloat16
    )
    grad32 = out_grad.astype(jnp.float32)
    partial_dots = jnp.stack([jnp.sum(grad32 * rows, axis=1) for rows in out_rows], axis=1)
    prob_grad = lax.psum(partial_dots, "loop")
    both = sum(w.astype(jnp.bfloat16) for w in wanted)
    input_grad = jnp.dot(both, back_dx, preferred_element_type=jnp.float32).astype(jnp.bfloat16)
    return (layer_out, input_grad, prob_grad, grad_gate, grad_up, grad_down)


def solution(mesh):
    in_specs = (
        P("dp", "loop"),
        P("dp", None),
        P("dp", None),
        P("dp", "loop"),
        P("dp", "loop", None),
        P("dp", "loop", None),
        P("dp", "loop", None),
    )
    out_specs = (
        P("dp", "loop"),
        P("dp", "loop"),
        P("dp", None),
        P("dp", "loop", None),
        P("dp", "loop", None),
        P("dp", "loop", None),
    )
    return jax.shard_map(shards, mesh=mesh, in_specs=in_specs, out_specs=out_specs, check_vma=False)
```

time: 581 us -> 388 us (0.67); the launches traced: 571 us -> 388 us
  waiting for transfers between devices: 342 us -> 170 us
  blocking collectives: 3.73 us -> 78.1 us
  local copies, waits for them, and re-layouts: 63.8 us -> 2.37 us
  other arithmetic: 34.8 us -> 1 us
  matrix products: 84.6 us -> 104 us
  starting transfers between devices: 28.4 us -> 17.7 us
    all_to_all x4 -> x3, waiting for transfers between devices: 302 us -> 162 us  [exchange(): moved = lax.all_to_all(cut, 'dp', split_axis=0, concat_axis=0, tiled=True)]
    all_to_all x0 -> x1, blocking collectives: none -> 75.1 us  [exchange(): moved = lax.all_to_all(cut, 'dp', split_axis=0, concat_axis=0, tiled=True)]
    all_gather x2, waiting for transfers between devices: 23.1 us -> 0.02 us  [the longest x1 0.02 us: shards(): rows_x = lax.all_gather(part_x, 'loop', axis=1, tiled=True)]
    mul x5 -> x0, local copies, waits for them, and re-layouts: 19.6 us -> none  [the longest x3 19.3 us: shards(): probs[:, :, None] * whole_g[:, None, :].astype(jnp.float32)]
    reduce_sum x3 -> x1, other arithmetic: 17.4 us -> 0.28 us  [shards(): jnp.sum(jnp.where(picks[k], probs[:, k][None, :], 0.0), axis=1)]
    dot_general x0 -> x6, matrix products: none -> 16.8 us  [the longest x2 7.24 us: shards(): jnp.dot(w.astype(jnp.bfloat16), back_out, preferred_element_type=jnp.floa...]
    scatter x1 -> x0, other arithmetic: 12.7 us -> none  [spread(): buffer = buffer.at[target].set(values.reshape(-1, width))]
    reduce_scatter x1, waiting for transfers between devices: 11.6 us -> 0.02 us  [shards(): lax.psum_scatter(out_part.astype(jnp.bfloat16), 'loop', scatter_dimension...]
  transfers between devices with their start and end apart: 8 -> 7, of which waited for: 8 -> 4; matrix products, arithmetic and copies ran while one was open for 19% -> 20% of each run, Pallas kernels for 0% -> 0%
where the time goes in v1:
time: 388 us
  waiting for transfers between devices  170 us (44%)
  matrix products  104 us (27%)
  blocking collectives  78.1 us (20%)
  starting transfers between devices  17.7 us (5%)
  between operations  13.9 us (4%)
    all_to_all x3, waiting for transfers between devices, exchange(): moved = lax.all_to_all(cut, 'dp', split_axis=0, concat_axis=0, tiled=True)  162 us
    all_to_all x1, blocking collectives, exchange(): moved = lax.all_to_all(cut, 'dp', split_axis=0, concat_axis=0, tiled=True)  75.1 us
    all_to_all x3, starting transfers between devices, exchange(): moved = lax.all_to_all(cut, 'dp', split_axis=0, concat_axis=0, tiled=True)  17.2 us
    dot_general x1, matrix products, shards(): lax.dot_general(rows_g, down_rows, contract, preferred_element_type=jnp.f...  11.6 us
    dot_general x1, matrix products, shards(): jnp.dot(dup, up_rows, preferred_element_type=jnp.float32)  11.3 us
    dot_general x1, matrix products, shards(): lax.dot_general(rows_x, gate_rows, contract, preferred_element_type=jnp.f...  10.5 us
    dot_general x1, matrix products, shards(): lax.dot_general(rows_x, up_rows, contract, preferred_element_type=jnp.flo...  10.2 us
    dot_general x1, matrix products, shards(): lax.dot_general(dgate, rows_x, outer, preferred_element_type=jnp.float32)  9.95 us
  transfers between devices with their start and end apart: 7, of which 4 were waited for; matrix products, arithmetic and copies ran while one was open for 20% of the time, Pallas kernels for 0%

profile of v1, /device:TPU:12, one launch (start us, length us, event | category | flops | bytes accessed | tf_op | source)
XLA Modules:
  0.0 387.6 jit_solution(5252909147177619072)
XLA Ops:
  7.2 0.9 copy.22
  8.1 0.1 eq.71
  8.2 0.3 fusion.16
  8.5 0.1 convert_element_type.63
  8.7 0.7 multiply_add_fusion
  9.5 2.7 convolution_convert_fusion.4
  12.1 7.3 %all-to-all-start = ((bf16[16,48,2048]{2,1,0:T(8,128)(2,1)}), bf16[16,48,2048]{2,1,0:T(8,128)(2,1)}, u32[]{:S(2)}, u32[]{:S(2)}) async-start(bf16[16,48,2048]{2,1,0:T(8,128)(2,1)} %bitcast.54), calls=%async_computation | async-start | bytes 6291456 | tf_op jit(solution)/shard_map/all_to_all | solution.py:34
  19.5 0.3 select_reduce_fusion
  19.8 2.7 multiply_convert_fusion
  22.4 67.5 %all-to-all-done = bf16[16,48,2048]{2,1,0:T(8,128)(2,1)} async-done(((bf16[16,48,2048]{2,1,0:T(8,128)(2,1)}), bf16[16,48,2048]{2,1,0:T(8,128)(2,1)}, u32[]{:S(2)}, u32[]{:S(2)}) %all-to-all-start) | async-done | bytes 3145760 | tf_op jit(solution)/shard_map/all_to_all | solution.py:34
  90.1 75.1 %all_to_all.20 = bf16[16,48,2048]{2,1,0:T(8,128)(2,1)} all-to-all(bf16[16,48,2048]{2,1,0:T(8,128)(2,1)} %bitcast.58), channel_id=1, replica_groups=mesh['loop'=2,'dp'=16] {'dp'}, dimensions={0} | all-to-all | bytes 6291456 | tf_op jit(solution)/shard_map/all_to_all | solution.py:34
  165.2 0.2 reduce-scatter.3.cloned.1.call-start
  165.4 10.2 %fusion.4 = f32[768,768]{1,0:T(8,128)} fusion(bf16[768,4096]{1,0:T(8,128)(2,1)} %all-gather.3.cloned.1.call-done, bf16[1,768,4096]{2,1,0:T(8,128)(2,1)} %param.12), kind=kOutput, calls=%fused_computation.9 | convolution fusion | flops 4831838208 | bytes 14942208 | tf_op jit(solution)/shard_map/dot_general | solution.py:47
  175.6 10.5 %fusion.8 = f32[768,768]{1,0:T(8,128)} fusion(bf16[768,4096]{1,0:T(8,128)(2,1)S(1)} %copy-done.3, bf16[1,768,4096]{2,1,0:T(8,128)(2,1)} %param.11), kind=kOutput, calls=%fused_computation.13 | convolution fusion | flops 4831838208 | bytes 14942208 | tf_op jit(solution)/shard_map/dot_general | solution.py:46
  186.1 11.6 %multiply_convert_fusion.1 = (bf16[768,768]{1,0:T(8,128)(2,1)S(1)}, bf16[768,768]{1,0:T(8,128)(2,1)}, bf16[768,768]{1,0:T(8,128)(2,1)S(1)}) fusion(f32[768,768]{1,0:T(8,128)} %fusion.8, f32[768,768]{1,0:T(8,128)} %fusion.4, bf16[768,4096]{1,0:T(8,128)(2,1)} %all-gather.5.cloned.1.call-done, bf16[1,768,4096]{2,1,0:T(8,128)(2,1)} %param.13), kind=kOutput, calls=%fused_computation.23 | convolution fusion | flops 4840685568 | bytes 20840448 | tf_op jit(solution)/shard_map/dot_general | solution.py:52
  197.7 1.1 copy-done.6
  198.8 9.9 %convolution_convert_fusion.3 = bf16[768,4096]{1,0:T(8,128)(2,1)} fusion(bf16[768,768]{1,0:T(8,128)(2,1)S(1)} %get-tuple-element.18, bf16[1,768,4096]{2,1,0:T(8,128)(2,1)} %param.13), kind=kOutput, calls=%fused_computation.4 | convolution fusion | flops 4834983936 | bytes 13762560 | tf_op jit(solution)/shard_map/dot_general | solution.py:51
  208.7 0.3 reduce-scatter.5.cloned.1.call-start
  208.9 7.5 %fusion.6 = f32[768,4096]{1,0:T(8,128)S(1)} fusion(bf16[768,768]{1,0:T(8,128)(2,1)} %get-tuple-element.17, bf16[1,768,4096]{2,1,0:T(8,128)(2,1)} %param.11), kind=kOutput, calls=%fused_computation.11 | convolution fusion | flops 4831838208 | bytes 20054016 | tf_op jit(solution)/shard_map/dot_general | solution.py:55
  216.4 11.3 %add_convert_fusion = bf16[768,4096]{1,0:T(8,128)(2,1)} fusion(f32[768,4096]{1,0:T(8,128)S(1)} %fusion.6, bf16[768,768]{1,0:T(8,128)(2,1)S(1)} %get-tuple-element.16, bf16[1,768,4096]{2,1,0:T(8,128)(2,1)} %param.12), kind=kOutput, calls=%fused_computation | convolution fusion | flops 4838129664 | bytes 26345472 | tf_op jit(solution)/shard_map/dot_general | solution.py:55
  227.8 5.1 %all-to-all-start.1 = ((bf16[16,48,2048]{2,1,0:T(8,128)(2,1)}), bf16[16,48,2048]{2,1,0:T(8,128)(2,1)}, u32[]{:S(2)}, u32[]{:S(2)}) async-start(bf16[16,48,2048]{2,1,0:T(8,128)(2,1)} %bitcast.57), calls=%async_computation.2 | async-start | bytes 6291456 | tf_op jit(solution)/shard_map/all_to_all | solution.py:34
  232.8 8.8 %reduce-scatter.5.cloned.1.call-done = bf16[768,2048]{1,0:T(8,128)(2,1)} async-done(((bf16[768,4096]{1,0:T(8,128)(2,1)}), bf16[768,2048]{1,0:T(8,128)(2,1)}) %reduce-scatter.5.cloned.1.call-update) | async-done | bytes 3145744 | tf_op jit(solution)/shard_map/reduce_scatter | solution.py:72
  241.6 60.8 %all-to-all-done.1 = bf16[16,48,2048]{2,1,0:T(8,128)(2,1)} async-done(((bf16[16,48,2048]{2,1,0:T(8,128)(2,1)}), bf16[16,48,2048]{2,1,0:T(8,128)(2,1)}, u32[]{:S(2)}, u32[]{:S(2)}) %all-to-all-start.1) | async-done | bytes 3145760 | tf_op jit(solution)/shard_map/all_to_all | solution.py:34
  302.4 4.8 %all-to-all-start.3 = ((bf16[16,48,2048]{2,1,0:T(8,128)(2,1)}), bf16[16,48,2048]{2,1,0:T(8,128)(2,1)}, u32[]{:S(2)}, u32[]{:S(2)}) async-start(bf16[16,48,2048]{2,1,0:T(8,128)(2,1)} %bitcast.56), calls=%async_computation.5 | async-start | bytes 6291456 | tf_op jit(solution)/shard_map/all_to_all | solution.py:34
  307.2 9.4 %fusion.12 = bf16[1,768,4096]{2,1,0:T(8,128)(2,1)} fusion(bf16[768,768]{1,0:T(8,128)(2,1)} %copy-done.6, bf16[768,4096]{1,0:T(8,128)(2,1)} %all-gather.5.cloned.1.call-done), kind=kOutput, calls=%fused_computation.18 | convolution fusion | flops 4834983936 | bytes 13762560 | tf_op jit(solution)/shard_map/dot_general | solution.py:65
  316.6 10.0 %fusion.10 = bf16[1,768,4096]{2,1,0:T(8,128)(2,1)} fusion(bf16[768,768]{1,0:T(8,128)(2,1)S(1)} %copy-done.5, bf16[768,4096]{1,0:T(8,128)(2,1)} %all-gather.3.cloned.1.call-done), kind=kOutput, calls=%fused_computation.16 | convolution fusion | flops 4834983936 | bytes 13762560 | tf_op jit(solution)/shard_map/dot_general | solution.py:59
  326.6 7.1 %fusion.11 = bf16[1,768,4096]{2,1,0:T(8,128)(2,1)} fusion(bf16[768,768]{1,0:T(8,128)(2,1)S(1)} %get-tuple-element.16, bf16[768,4096]{1,0:T(8,128)(2,1)S(1)} %bitcast.76), kind=kOutput, calls=%fused_computation.17 | convolution fusion | flops 4834983936 | bytes 13762560 | tf_op jit(solution)/shard_map/dot_general | solution.py:62
  333.7 2.9 fusion.18
  336.6 4.3 %fusion.14 = (f32[256]{0:T(256)S(1)}, f32[256]{0:T(256)S(1)}, bf16[256,2048]{1,0:T(8,128)(2,1)}) fusion(bf16[256,2048]{1,0:T(8,128)(2,1)S(1)} %copy-done.4, f32[256,2048]{1,0:T(8,128)S(1)} %fusion.18, f32[256]{0:T(256)S(1)} %bitcast.70, f32[256]{0:T(256)S(1)} %bitcast.72, bf16[768,2048]{1,0:T(8,128)(2,1)} %bitcast.10, s32[256]{0:T(256)S(1)} %bitcast.67), kind=kOutput, calls=%fused_computation.28 | convolution fusion | flops 810221056 | bytes 7345152 | tf_op jit(solution)/shard_map/dot_general | solution.py:79
  340.9 3.0 psum.7
  344.0 33.2 %all-to-all-done.3 = bf16[16,48,2048]{2,1,0:T(8,128)(2,1)} async-done(((bf16[16,48,2048]{2,1,0:T(8,128)(2,1)}), bf16[16,48,2048]{2,1,0:T(8,128)(2,1)}, u32[]{:S(2)}, u32[]{:S(2)}) %all-to-all-start.3) | async-done | bytes 3145760 | tf_op jit(solution)/shard_map/all_to_all | solution.py:34
  377.2 3.9 %convolution_convert_fusion.5 = bf16[256,2048]{1,0:T(8,128)(2,1)} fusion(bf16[768,2048]{1,0:T(8,128)(2,1)} %bitcast.14, s32[256]{0:T(256)S(1)} %bitcast.63, s32[256]{0:T(256)S(1)} %bitcast.68), kind=kOutput, calls=%fused_computation.22 | convolution fusion | flops 807403520 | bytes 4196352 | tf_op jit(solution)/shard_map/dot_general | solution.py:89
  (33 shorter events, 0.3 us)
Async XLA Ops:
  7.2 2.3 copy-start
  12.1 7.4 %copy-start.2 = (f32[256,2]{0,1:T(2,128)S(1)}, f32[256,2]{0,1:T(2,128)}, u32[]{:S(2)}) copy-start(f32[256,2]{0,1:T(2,128)} %param.8) | copy-start | bytes 6148
  12.1 7.7 %copy-start.4 = (bf16[256,2048]{1,0:T(8,128)(2,1)S(1)}, bf16[256,2048]{1,0:T(8,128)(2,1)}, u32[]{:S(2)}) copy-start(bf16[256,2048]{1,0:T(8,128)(2,1)} %param.10) | copy-start | bytes 3145732
  12.1 77.9 %all-to-all-start = ((bf16[16,48,2048]{2,1,0:T(8,128)(2,1)}), bf16[16,48,2048]{2,1,0:T(8,128)(2,1)}, u32[]{:S(2)}, u32[]{:S(2)}) async-start(bf16[16,48,2048]{2,1,0:T(8,128)(2,1)} %bitcast.54), calls=%async_computation | async-start | bytes 6291456 | tf_op jit(solution)/shard_map/all_to_all | solution.py:34
  19.4 146.0 %all-gather.3.cloned.1.call-start = ((), (), s32[]{:S(2)}) async-start(), calls=%async_computation.6 | async-start | bytes 9437184 | tf_op jit(solution)/shard_map/all_gather | solution.py:40
  90.0 96.1 %all-gather.5.cloned.1.call-start = ((), (), s32[]{:S(2)}) async-start(), calls=%async_computation.8 | async-start | bytes 9437184 | tf_op jit(solution)/shard_map/all_gather | solution.py:41
  165.2 62.6 %reduce-scatter.3.cloned.1.call-start = ((), (), s32[]{:S(2)}) async-start(), calls=%async_computation.7 | async-start | bytes 9437184 | tf_op jit(solution)/shard_map/reduce_scatter | solution.py:68
  165.4 10.2 %copy-start.3 = (bf16[768,4096]{1,0:T(8,128)(2,1)S(1)}, bf16[768,4096]{1,0:T(8,128)(2,1)}, u32[]{:S(2)}) copy-start(bf16[768,4096]{1,0:T(8,128)(2,1)} %all-gather.3.cloned.1.call-done) | copy-start | bytes 18874372
  197.7 1.1 copy-start.6
  208.7 33.0 %reduce-scatter.5.cloned.1.call-start = ((), (), s32[]{:S(2)}) async-start(), calls=%async_computation.9 | async-start | bytes 9437184 | tf_op jit(solution)/shard_map/reduce_scatter | solution.py:72
  227.8 74.6 %all-to-all-start.1 = ((bf16[16,48,2048]{2,1,0:T(8,128)(2,1)}), bf16[16,48,2048]{2,1,0:T(8,128)(2,1)}, u32[]{:S(2)}, u32[]{:S(2)}) async-start(bf16[16,48,2048]{2,1,0:T(8,128)(2,1)} %bitcast.57), calls=%async_computation.2 | async-start | bytes 6291456 | tf_op jit(solution)/shard_map/all_to_all | solution.py:34
  302.4 74.8 %all-to-all-start.3 = ((bf16[16,48,2048]{2,1,0:T(8,128)(2,1)}), bf16[16,48,2048]{2,1,0:T(8,128)(2,1)}, u32[]{:S(2)}, u32[]{:S(2)}) async-start(bf16[16,48,2048]{2,1,0:T(8,128)(2,1)} %bitcast.56), calls=%async_computation.5 | async-start | bytes 6291456 | tf_op jit(solution)/shard_map/all_to_all | solution.py:34
  307.2 9.4 %copy-start.5 = (bf16[768,768]{1,0:T(8,128)(2,1)S(1)}, bf16[768,768]{1,0:T(8,128)(2,1)}, u32[]{:S(2)}) copy-start(bf16[768,768]{1,0:T(8,128)(2,1)} %get-tuple-element.17) | copy-start | bytes 3538948
  307.2 19.3 %slice-start = ((s8[6291456]{0:T(1024)(128)(4,1)}), s8[4194304]{0:T(1024)(128)(4,1)S(1)}, s32[]{:S(2)}) async-start(s8[6291456]{0:T(1024)(128)(4,1)} %bitcast.75), calls=%async_computation.10 | async-start | bytes 8388608
  316.6 10.0 %slice-start.1 = ((s8[6291456]{0:T(1024)(128)(4,1)}), s8[2097152]{0:T(1024)(128)(4,1)S(1)}, s32[]{:S(2)}) async-start(s8[6291456]{0:T(1024)(128)(4,1)} %bitcast.75), calls=%async_computation.11 | async-start | bytes 4194304
  336.6 44.5 %copy-start.1 = (bf16[256,2048]{1,0:T(8,128)(2,1)S(1)}, bf16[256,2048]{1,0:T(8,128)(2,1)}, u32[]{:S(2)}) copy-start(bf16[256,2048]{1,0:T(8,128)(2,1)} %param.7) | copy-start | bytes 3145732
Sparse Core Ops, SparseCore 0:
  90.1 16.4 all-gather.2
  165.3 16.1 all-gather.4
  208.8 13.8 reduce-scatter.2
  227.9 13.7 reduce-scatter.4

commit v2 on v1

--- a/solution.py
+++ b/solution.py
@@ -1,7 +1,210 @@
+import functools
+
 import jax
 import jax.numpy as jnp
 from jax import lax
+from jax.experimental import pallas as pl
+from jax.experimental.pallas import tpu as pltpu
 from jax.sharding import PartitionSpec as P
+
+BF = jnp.bfloat16
+F32 = jnp.float32
+CONTRACT = (((1,), (1,)), ((), ()))
+STEP = 256
+WIDE = 512
+
+
+def middle(
+    n, send_x, send_g, w_gate, w_up, w_down,
+    full_x, full_g, hidden, dgate, dup, back_out, dx_sum,
+    wg, wu, wd, fact_gate, fact_up, out_own, to_mate, mate_out, mate_dx,
+    x_out, x_in, xm_out, xm_in, g_out, g_in, gm_out, gm_in, o_out, o_in,
+    mate_send, mate_recv, local_sem,
+):
+    me = lax.axis_index("dp")
+    side = lax.axis_index("loop")
+    mate = 1 - side
+    cap, part = send_x.shape[1:]
+    rows = n * cap
+    units = wg.shape[0]
+    mine = pl.ds(pl.multiple_of(side * part, part), part)
+
+    def peer(step):
+        return lax.rem(me + step, n)
+
+    def source(step):
+        return lax.rem(me - step + n, n)
+
+    def over_dp(src, dst, out_sem, in_sem, step):
+        return pltpu.make_async_remote_copy(
+            src_ref=src, dst_ref=dst, send_sem=out_sem.at[step], recv_sem=in_sem.at[step],
+            device_id={"dp": peer(step)}, device_id_type=pl.DeviceIdType.MESH,
+        )
+
+    def over_loop(src, dst, out_sem, in_sem, step):
+        return pltpu.make_async_remote_copy(
+            src_ref=src, dst_ref=dst, send_sem=out_sem.at[step], recv_sem=in_sem.at[step],
+            device_id={"loop": mate}, device_id_type=pl.DeviceIdType.MESH,
+        )
+
+    def x_copy(step):
+        return over_dp(send_x.at[peer(step)], full_x.at[me, :, mine], x_out, x_in, step)
+
+    def g_copy(step):
+        return over_dp(send_g.at[peer(step)], full_g.at[me, :, mine], g_out, g_in, step)
+
+    def o_copy(step):
+        return over_dp(out_own.at[peer(step)], back_out.at[me], o_out, o_in, step)
+
+    def handed(full, step, out_sem, in_sem):
+        at = full.at[source(step), :, mine]
+        return over_loop(at, at, out_sem, in_sem, step)
+
+    barrier = pltpu.get_barrier_semaphore()
+
+    @pl.loop(1, n)
+    def _(step):
+        pl.semaphore_signal(
+            barrier, inc=1, device_id={"dp": peer(step)}, device_id_type=pl.DeviceIdType.MESH
+        )
+
+    pl.semaphore_signal(
+        barrier, inc=1, device_id={"loop": mate}, device_id_type=pl.DeviceIdType.MESH
+    )
+    pl.semaphore_wait(barrier, n)
+
+    @pl.loop(1, n)
+    def _(step):
+        x_copy(step).start()
+
+    own_x = pltpu.make_async_copy(send_x.at[me], full_x.at[me, :, mine], local_sem.at[0])
+    own_g = pltpu.make_async_copy(send_g.at[me], full_g.at[me, :, mine], local_sem.at[1])
+    weights = [
+        pltpu.make_async_copy(src, dst, local_sem.at[2 + i])
+        for i, (src, dst) in enumerate(((w_gate, wg), (w_up, wu), (w_down, wd)))
+    ]
+    own_x.start()
+    own_g.start()
+    for copy in weights:
+        copy.start()
+    own_x.wait()
+    own_g.wait()
+    handed(full_x, 0, xm_out, xm_in).start()
+    handed(full_g, 0, gm_out, gm_in).start()
+
+    @pl.loop(1, n)
+    def _(step):
+        x_copy(step).wait()
+        handed(full_x, step, xm_out, xm_in).start()
+        g_copy(step).start()
+
+    for copy in weights:
+        copy.wait()
+
+    @pl.loop(0, n)
+    def _(step):
+        handed(full_x, step, xm_out, xm_in).wait()
+
+    @pl.loop(0, units // STEP)
+    def _(i):
+        at = pl.ds(pl.multiple_of(i * STEP, STEP), STEP)
+        x = full_x[...].reshape(rows, 2 * part)
+        gate = lax.dot_general(x, wg[at, :], CONTRACT, preferred_element_type=F32)
+        up = lax.dot_general(x, wu[at, :], CONTRACT, preferred_element_type=F32)
+        sig = jax.nn.sigmoid(gate)
+        silu = gate * sig
+        hidden[:, at] = (silu * up).astype(BF)
+        fact_up[:, at] = silu
+        fact_gate[:, at] = up * sig * (1.0 + gate * (1.0 - sig))
+
+    def fill(dst, which, product):
+        @pl.loop(0, part // WIDE)
+        def _(i):
+            first = pl.multiple_of(i * WIDE, WIDE)
+            at = pl.ds(pl.multiple_of(which * part + first, WIDE), WIDE)
+            dst[:, :, pl.ds(first, WIDE)] = product(at).astype(BF).reshape(n, cap, WIDE)
+
+    def add(dst, other):
+        @pl.loop(0, n)
+        def _(i):
+            dst[i] = (dst[i].astype(F32) + other[i].astype(F32)).astype(BF)
+
+    def out_product(at):
+        return jnp.dot(hidden[...], wd[:, at], preferred_element_type=F32)
+
+    fill(to_mate, mate, out_product)
+    swap_out = over_loop(to_mate, mate_out, mate_send, mate_recv, 0)
+    swap_out.start()
+    fill(out_own, side, out_product)
+    swap_out.wait()
+    add(out_own, mate_out)
+
+    @pl.loop(1, n)
+    def _(step):
+        g_copy(step).wait()
+        handed(full_g, step, gm_out, gm_in).start()
+        o_copy(step).start()
+
+    own_out = pltpu.make_async_copy(out_own.at[me], back_out.at[me], local_sem.at[5])
+    own_out.start()
+
+    @pl.loop(0, n)
+    def _(step):
+        handed(full_g, step, gm_out, gm_in).wait()
+
+    @pl.loop(0, units // STEP)
+    def _(i):
+        at = pl.ds(pl.multiple_of(i * STEP, STEP), STEP)
+        g = full_g[...].reshape(rows, 2 * part)
+        dhid = lax.dot_general(g, wd[at, :], CONTRACT, preferred_element_type=F32)
+        dgate[:, at] = (dhid * fact_gate[:, at]).astype(BF)
+        dup[:, at] = (dhid * fact_up[:, at]).astype(BF)
+
+    def dx_product(at):
+        return jnp.dot(dgate[...], wg[:, at], preferred_element_type=F32) + jnp.dot(
+            dup[...], wu[:, at], preferred_element_type=F32
+        )
+
+    fill(to_mate, mate, dx_product)
+    swap_dx = over_loop(to_mate, mate_dx, mate_send, mate_recv, 1)
+    swap_dx.start()
+    fill(dx_sum, side, dx_product)
+    swap_dx.wait()
+    add(dx_sum, mate_dx)
+    own_out.wait()
+
+    @pl.loop(1, n)
+    def _(step):
+        o_copy(step).wait()
+
+
+def run_middle(send_x, send_g, w_gate, w_up, w_down):
+    n, cap, part = send_x.shape
+    units, width = w_gate.shape
+    rows = n * cap
+    vmem = pl.BlockSpec(memory_space=pltpu.VMEM)
+    hbm = pl.BlockSpec(memory_space=pl.ANY)
+    half = jax.ShapeDtypeStruct((n, cap, part), BF)
+    full = jax.ShapeDtypeStruct((n, cap, width), BF)
+    acts = jax.ShapeDtypeStruct((rows, units), BF)
+    dma = pltpu.SemaphoreType.DMA
+    return pl.pallas_call(
+        functools.partial(middle, n),
+        out_shape=(full, full, acts, acts, acts, half, half),
+        in_specs=[hbm] * 5,
+        out_specs=(vmem, vmem, vmem, vmem, vmem, hbm, vmem),
+        scratch_shapes=[pltpu.VMEM((units, width), BF)] * 3
+        + [pltpu.VMEM((rows, units), F32)] * 2
+        + [pltpu.VMEM((n, cap, part), BF)] * 4
+        + [dma((n,))] * 10
+        + [dma((2,)), dma((2,)), dma((6,))],
+        compiler_params=pltpu.CompilerParams(
+            collective_id=0, has_side_effects=True, vmem_limit_bytes=61 * 1024 * 1024
+        ),
+        cost_estimate=pl.CostEstimate(
+            flops=12 * rows * units * width, bytes_accessed=60_000_000, transcendentals=rows * units
+        ),
+    )(send_x, send_g, w_gate, w_up, w_down)
 
 
 def shards(tokens, probs, routes, out_grad, w_gate, w_up, w_down):
@@ -34,27 +237,41 @@
         moved = lax.all_to_all(cut, "dp", split_axis=0, concat_axis=0, tiled=True)
         return moved.reshape(experts * capacity, rows.shape[-1])
 
-    part_x = exchange(send_x)
-    part_x, send_g = lax.optimization_barrier((part_x, send_g))
-    part_g = exchange(send_g)
-    rows_x = lax.all_gather(part_x, "loop", axis=1, tiled=True)
-    rows_g = lax.all_gather(part_g, "loop", axis=1, tiled=True)
-    gate_rows = w_gate[0]
-    up_rows = w_up[0]
-    down_rows = w_down[0]
-    contract = (((1,), (1,)), ((), ()))
-    gate = lax.dot_general(rows_x, gate_rows, contract, preferred_element_type=jnp.float32)
-    up = lax.dot_general(rows_x, up_rows, contract, preferred_element_type=jnp.float32)
-    sig = jax.nn.sigmoid(gate)
-    silu = gate * sig
-    hidden = (silu * up).astype(jnp.bfloat16)
-    out_part = jnp.dot(hidden, down_rows, preferred_element_type=jnp.float32)
-    dhid = lax.dot_general(rows_g, down_rows, contract, preferred_element_type=jnp.float32)
-    dgate = (dhid * up * sig * (1.0 + gate * (1.0 - sig))).astype(jnp.bfloat16)
-    dup = (dhid * silu).astype(jnp.bfloat16)
-    dx_part = jnp.dot(dgate, gate_rows, preferred_element_type=jnp.float32) + jnp.dot(
-        dup, up_rows, preferred_element_type=jnp.float32
-    )
+    if lax.axis_size("loop") == 2:
+        shape = (experts, capacity, tokens.shape[1])
+        rows_x, rows_g, hidden, dgate, dup, back_out, dx_sum = run_middle(
+            send_x.reshape(shape), send_g.reshape(shape), w_gate[0], w_up[0], w_down[0]
+        )
+        rows_x = rows_x.reshape(experts * capacity, -1)
+        rows_g = rows_g.reshape(experts * capacity, -1)
+        back_out = back_out.reshape(experts * capacity, -1)
+        dx_sum = dx_sum.reshape(experts * capacity, -1)
+    else:
+        part_x = exchange(send_x)
+        part_x, send_g = lax.optimization_barrier((part_x, send_g))
+        part_g = exchange(send_g)
+        rows_x = lax.all_gather(part_x, "loop", axis=1, tiled=True)
+        rows_g = lax.all_gather(part_g, "loop", axis=1, tiled=True)
+        gate_rows = w_gate[0]
+        up_rows = w_up[0]
+        down_rows = w_down[0]
+        contract = (((1,), (1,)), ((), ()))
+        gate = lax.dot_general(rows_x, gate_rows, contract, preferred_element_type=jnp.float32)
+        up = lax.dot_general(rows_x, up_rows, contract, preferred_element_type=jnp.float32)
+        sig = jax.nn.sigmoid(gate)
+        silu = gate * sig
+        hidden = (silu * up).astype(jnp.bfloat16)
+        out_part = jnp.dot(hidden, down_rows, preferred_element_type=jnp.float32)
+        dhid = lax.dot_general(rows_g, down_rows, contract, preferred_element_type=jnp.float32)
+        dgate = (dhid * up * sig * (1.0 + gate * (1.0 - sig))).astype(jnp.bfloat16)
+        dup = (dhid * silu).astype(jnp.bfloat16)
+        dx_part = jnp.dot(dgate, gate_rows, preferred_element_type=jnp.float32) + jnp.dot(
+            dup, up_rows, preferred_element_type=jnp.float32
+        )
+        outs = lax.psum_scatter(out_part.astype(BF), "loop", scatter_dimension=1, tiled=True)
+        back_out = exchange(outs)
+        dx_sum = lax.psum_scatter(dx_part.astype(BF), "loop", scatter_dimension=1, tiled=True)
+    back_dx = exchange(dx_sum)
     outer = (((0,), (0,)), ((), ()))
     grad_gate = lax.dot_general(dgate, rows_x, outer, preferred_element_type=jnp.float32).astype(
         jnp.bfloat16
@@ -65,15 +282,6 @@
     grad_down = lax.dot_general(hidden, rows_g, outer, preferred_element_type=jnp.float32).astype(
         jnp.bfloat16
     )[None]
-    out_sum = lax.psum_scatter(
-        out_part.astype(jnp.bfloat16), "loop", scatter_dimension=1, tiled=True
-    )
-    back_out = exchange(out_sum)
-    dx_sum = lax.psum_scatter(
-        dx_part.astype(jnp.bfloat16), "loop", scatter_dimension=1, tiled=True
-    )
-    back_out, dx_sum = lax.optimization_barrier((back_out, dx_sum))
-    back_dx = exchange(dx_sum)
     wanted = [(target[:, k][:, None] == slots[None, :]) for k in range(top_count)]
     out_rows = [
         jnp.dot(w.astype(jnp.bfloat16), back_out, preferred_element_type=jnp.float32)

time: 388 us -> 324 us (0.84)
  Pallas kernels: 0 us -> 232 us
  waiting for transfers between devices: 170 us -> 34.4 us
  blocking collectives: 78.1 us -> 3.04 us
  matrix products: 104 us -> 42 us
  between operations: 13.9 us -> 0.75 us
  starting transfers between devices: 17.7 us -> 8.04 us
    pallas_call x0 -> x1, Pallas kernels: none -> 232 us  [run_middle(): pl.pallas_call(functools.partial(middle, n), out_shape=(full, full, acts,...]
    all_to_all x3 -> x1, waiting for transfers between devices: 162 us -> 34.4 us  [exchange(): moved = lax.all_to_all(cut, 'dp', split_axis=0, concat_axis=0, tiled=True)]
    all_to_all x1 -> x0, blocking collectives: 75.1 us -> none  [exchange(): moved = lax.all_to_all(cut, 'dp', split_axis=0, concat_axis=0, tiled=True)]
    dot_general x6 -> x0, matrix products: 60.9 us -> none  [the longest x1 11.6 us: shards(): lax.dot_general(rows_g, down_rows, contract, preferred_element_type=jnp.f...]
    all_to_all x3 -> x1, starting transfers between devices: 17.2 us -> 8.04 us  [exchange(): moved = lax.all_to_all(cut, 'dp', split_axis=0, concat_axis=0, tiled=True)]
    reduce_scatter x2 -> x0, waiting for transfers between devices: 8.83 us -> none  [the longest x1 8.81 us: shards(): lax.psum_scatter(dx_part.astype(jnp.bfloat16), 'loop', scatter_dimension=...]
  transfers between devices with their start and end apart: 7 -> 1, of which waited for: 4 -> 1; matrix products, arithmetic and copies ran while one was open for 20% -> 10% of each run, Pallas kernels for 0% -> 0%
where the time goes in v2:
time: 324 us; the launch traced here: 323 us
  Pallas kernels  232 us (72%)
  matrix products  42 us (13%)
  waiting for transfers between devices  34.4 us (11%)
  starting transfers between devices  8.04 us (2%)
    pallas_call x1, Pallas kernels, run_middle(): pl.pallas_call(functools.partial(middle, n), out_shape=(full, full, acts,...  232 us
    all_to_all x1, waiting for transfers between devices, exchange(): moved = lax.all_to_all(cut, 'dp', split_axis=0, concat_axis=0, tiled=True)  34.4 us
    dot_general x1, matrix products, shards(): lax.dot_general(dup, rows_x, outer, preferred_element_type=jnp.float32)  9.96 us
    dot_general x1, matrix products, shards(): lax.dot_general(dgate, rows_x, outer, preferred_element_type=jnp.float32)  9.95 us
    all_to_all x1, starting transfers between devices, exchange(): moved = lax.all_to_all(cut, 'dp', split_axis=0, concat_axis=0, tiled=True)  8.04 us
    dot_general x1, matrix products, shards(): lax.dot_general(hidden, rows_g, outer, preferred_element_type=jnp.float32)  7.08 us
  transfers between devices with their start and end apart: 1, of which 1 were waited for; matrix products, arithmetic and copies ran while one was open for 10% of the time, Pallas kernels for 0%

profile of v2, /device:TPU:12, one launch (start us, length us, event | category | flops | bytes accessed | tf_op | source)
XLA Modules:
  0.0 323.3 jit_solution(7866760406205042045)
XLA Ops:
  0.6 0.0 copy-start
  0.6 0.8 fusion.27
  1.4 0.8 copy.22
  2.3 0.1 eq.71
  2.4 0.3 fusion.5
  2.7 0.1 convert_element_type.48
  2.8 0.1 copy.23
  2.9 0.7 multiply_add_fusion
  3.6 0.0 copy-done
  3.6 2.7 convolution_convert_fusion.3
  6.3 0.3 select_reduce_fusion
  6.6 0.0 copy-done.3
  6.6 2.7 multiply_convert_fusion
  9.2 232.1 %shard_map.118 = (bf16[16,48,4096]{2,1,0:T(8,128)(2,1)}, bf16[16,48,4096]{2,1,0:T(8,128)(2,1)}, bf16[768,768]{1,0:T(8,128)(2,1)}, bf16[768,768]{1,0:T(8,128)(2,1...) custom-call(bf16[16,48,2048]{2,1,0:T(8,128)(2,1)} %bitcast.32, ...), custom_call_target="tpu_custom_call" | custom-call | flops 28991029248 | bytes 60000000 | tf_op jit(solution)/shard_map/pallas_call | solution.py:191
  241.3 8.0 %all-to-all-start = ((bf16[16,48,2048]{2,1,0:T(8,128)(2,1)}), bf16[16,48,2048]{2,1,0:T(8,128)(2,1)}, u32[]{:S(2)}, u32[]{:S(2)}) async-start(bf16[16,48,2048]{2,1,0:T(8,128)(2,1)} %get-tuple-element.14), calls=%async_computation | async-start | bytes 6291456 | tf_op jit(solution)/shard_map/all_to_all | solution.py:237
  249.4 3.1 fusion.7
  252.4 0.0 copy-done.2
  252.4 0.0 copy-start.6
  252.5 2.4 fusion.3
  254.9 3.0 psum.7
  257.9 0.0 copy-done.6
  257.9 9.9 %fusion = bf16[1,768,4096]{2,1,0:T(8,128)(2,1)} fusion(bf16[768,768]{1,0:T(8,128)(2,1)S(1)} %copy-done.6, bf16[768,4096]{1,0:T(8,128)(2,1)} %bitcast.57), kind=kOutput, calls=%fused_computation.4 | convolution fusion | flops 4834983936 | bytes 13762560 | tf_op jit(solution)/shard_map/dot_general | solution.py:276
  267.9 0.0 copy-done.5
  267.9 10.0 %fusion.1 = bf16[1,768,4096]{2,1,0:T(8,128)(2,1)} fusion(bf16[768,768]{1,0:T(8,128)(2,1)S(1)} %copy-done.5, bf16[768,4096]{1,0:T(8,128)(2,1)} %bitcast.58), kind=kOutput, calls=%fused_computation.5 | convolution fusion | flops 4834983936 | bytes 13762560 | tf_op jit(solution)/shard_map/dot_general | solution.py:279
  277.8 0.0 slice-done
  277.8 0.0 slice-done.1
  277.8 0.0 copy-done.4
  277.9 0.0 copy-start.1
  277.9 7.1 %fusion.2 = bf16[1,768,4096]{2,1,0:T(8,128)(2,1)} fusion(bf16[768,768]{1,0:T(8,128)(2,1)S(1)} %copy-done.4, bf16[768,4096]{1,0:T(8,128)(2,1)S(1)} %bitcast.56), kind=kOutput, calls=%fused_computation.6 | convolution fusion | flops 4834983936 | bytes 13762560 | tf_op jit(solution)/shard_map/dot_general | solution.py:282
  284.9 34.4 %all-to-all-done = bf16[16,48,2048]{2,1,0:T(8,128)(2,1)} async-done(((bf16[16,48,2048]{2,1,0:T(8,128)(2,1)}), bf16[16,48,2048]{2,1,0:T(8,128)(2,1)}, u32[]{:S(2)}, u32[]{:S(2)}) %all-to-all-start) | async-done | bytes 3145760 | tf_op jit(solution)/shard_map/all_to_all | solution.py:237
  319.3 3.9 %convolution_convert_fusion.4 = bf16[256,2048]{1,0:T(8,128)(2,1)} fusion(bf16[768,2048]{1,0:T(8,128)(2,1)} %bitcast.10, s32[256]{0:T(256)S(1)} %bitcast.39, s32[256]{0:T(256)S(1)} %bitcast.44), kind=kOutput, calls=%fused_computation.10 | convolution fusion | flops 807403520 | bytes 4196352 | tf_op jit(solution)/shard_map/dot_general | solution.py:297
  323.3 0.0 copy-done.1
  (11 shorter events, 0.0 us)
Async XLA Ops:
  0.6 3.0 copy-start
  3.6 3.0 copy-start.3
  241.3 78.0 %all-to-all-start = ((bf16[16,48,2048]{2,1,0:T(8,128)(2,1)}), bf16[16,48,2048]{2,1,0:T(8,128)(2,1)}, u32[]{:S(2)}, u32[]{:S(2)}) async-start(bf16[16,48,2048]{2,1,0:T(8,128)(2,1)} %get-tuple-element.14), calls=%async_computation | async-start | bytes 6291456 | tf_op jit(solution)/shard_map/all_to_all | solution.py:237
  249.4 3.1 copy-start.2
  252.4 5.5 %copy-start.6 = (bf16[768,768]{1,0:T(8,128)(2,1)S(1)}, bf16[768,768]{1,0:T(8,128)(2,1)}, u32[]{:S(2)}) copy-start(bf16[768,768]{1,0:T(8,128)(2,1)} %get-tuple-element.15) | copy-start | bytes 3538948
  257.9 10.0 %copy-start.5 = (bf16[768,768]{1,0:T(8,128)(2,1)S(1)}, bf16[768,768]{1,0:T(8,128)(2,1)}, u32[]{:S(2)}) copy-start(bf16[768,768]{1,0:T(8,128)(2,1)} %get-tuple-element.17) | copy-start | bytes 3538948
  257.9 19.9 %slice-start = ((s8[6291456]{0:T(1024)(128)(4,1)}), s8[4194304]{0:T(1024)(128)(4,1)S(1)}, s32[]{:S(2)}) async-start(s8[6291456]{0:T(1024)(128)(4,1)} %bitcast.54), calls=%async_computation.1 | async-start | bytes 8388608
  267.9 10.0 %slice-start.1 = ((s8[6291456]{0:T(1024)(128)(4,1)}), s8[2097152]{0:T(1024)(128)(4,1)S(1)}, s32[]{:S(2)}) async-start(s8[6291456]{0:T(1024)(128)(4,1)} %bitcast.54), calls=%async_computation.2 | async-start | bytes 4194304
  267.9 10.0 %copy-start.4 = (bf16[768,768]{1,0:T(8,128)(2,1)S(1)}, bf16[768,768]{1,0:T(8,128)(2,1)}, u32[]{:S(2)}) copy-start(bf16[768,768]{1,0:T(8,128)(2,1)} %get-tuple-element.18) | copy-start | bytes 3538948
  277.9 45.4 %copy-start.1 = (bf16[256,2048]{1,0:T(8,128)(2,1)S(1)}, bf16[256,2048]{1,0:T(8,128)(2,1)}, u32[]{:S(2)}) copy-start(bf16[256,2048]{1,0:T(8,128)(2,1)} %param.7) | copy-start | bytes 3145732

commit v3 on v2

--- a/solution.py
+++ b/solution.py
@@ -27,6 +27,7 @@
     cap, part = send_x.shape[1:]
     rows = n * cap
     units = wg.shape[0]
+    ahead = n // 8
     mine = pl.ds(pl.multiple_of(side * part, part), part)
 
     def peer(step):
@@ -76,6 +77,10 @@
     @pl.loop(1, n)
     def _(step):
         x_copy(step).start()
+
+    @pl.loop(1, 1 + ahead)
+    def _(step):
+        g_copy(step).start()
 
     own_x = pltpu.make_async_copy(send_x.at[me], full_x.at[me, :, mine], local_sem.at[0])
     own_g = pltpu.make_async_copy(send_g.at[me], full_g.at[me, :, mine], local_sem.at[1])
@@ -96,7 +101,10 @@
     def _(step):
         x_copy(step).wait()
         handed(full_x, step, xm_out, xm_in).start()
-        g_copy(step).start()
+
+        @pl.when(step + ahead < n)
+        def _():
+            g_copy(step + ahead).start()
 
     for copy in weights:
         copy.wait()
@@ -139,11 +147,18 @@
     swap_out.wait()
     add(out_own, mate_out)
 
+    @pl.loop(1, 1 + ahead)
+    def _(step):
+        o_copy(step).start()
+
     @pl.loop(1, n)
     def _(step):
         g_copy(step).wait()
         handed(full_g, step, gm_out, gm_in).start()
-        o_copy(step).start()
+
+        @pl.when(step + ahead < n)
+        def _():
+            o_copy(step + ahead).start()
 
     own_out = pltpu.make_async_copy(out_own.at[me], back_out.at[me], local_sem.at[5])
     own_out.start()

time: 324 us -> 322 us (level)
  no operation moved by 1% of the time
where the time goes in v3:
time: 322 us
  Pallas kernels  231 us (72%)
  matrix products  42 us (13%)
  waiting for transfers between devices  34.4 us (11%)
  starting transfers between devices  8.04 us (2%)
    pallas_call x1, Pallas kernels, run_middle(): pl.pallas_call(functools.partial(middle, n), out_shape=(full, full, acts,...  231 us
    all_to_all x1, waiting for transfers between devices, exchange(): moved = lax.all_to_all(cut, 'dp', split_axis=0, concat_axis=0, tiled=True)  34.4 us
    dot_general x1, matrix products, shards(): lax.dot_general(dup, rows_x, outer, preferred_element_type=jnp.float32)  9.96 us
    dot_general x1, matrix products, shards(): lax.dot_general(dgate, rows_x, outer, preferred_element_type=jnp.float32)  9.95 us
    all_to_all x1, starting transfers between devices, exchange(): moved = lax.all_to_all(cut, 'dp', split_axis=0, concat_axis=0, tiled=True)  8.04 us
    dot_general x1, matrix products, shards(): lax.dot_general(hidden, rows_g, outer, preferred_element_type=jnp.float32)  7.08 us
  transfers between devices with their start and end apart: 1, of which 1 were waited for; matrix products, arithmetic and copies ran while one was open for 10% of the time, Pallas kernels for 0%

profile of v3, /device:TPU:12, one launch (start us, length us, event | category | flops | bytes accessed | tf_op | source)
XLA Modules:
  0.0 321.7 jit_solution(2350022619546224610)
XLA Ops:
  0.6 0.0 copy-start
  0.6 0.8 fusion.27
  1.4 0.8 copy.22
  2.3 0.1 eq.71
  2.4 0.3 fusion.5
  2.7 0.1 convert_element_type.48
  2.8 0.1 copy.23
  2.9 0.7 multiply_add_fusion
  3.6 0.0 copy-done
  3.6 2.7 convolution_convert_fusion.3
  6.3 0.3 select_reduce_fusion
  6.6 0.0 copy-done.3
  6.6 2.7 multiply_convert_fusion
  9.2 230.5 %shard_map.118 = (bf16[16,48,4096]{2,1,0:T(8,128)(2,1)}, bf16[16,48,4096]{2,1,0:T(8,128)(2,1)}, bf16[768,768]{1,0:T(8,128)(2,1)}, bf16[768,768]{1,0:T(8,128)(2,1...) custom-call(bf16[16,48,2048]{2,1,0:T(8,128)(2,1)} %bitcast.32, ...), custom_call_target="tpu_custom_call" | custom-call | flops 28991029248 | bytes 60000000 | tf_op jit(solution)/shard_map/pallas_call | solution.py:206
  239.8 8.0 %all-to-all-start = ((bf16[16,48,2048]{2,1,0:T(8,128)(2,1)}), bf16[16,48,2048]{2,1,0:T(8,128)(2,1)}, u32[]{:S(2)}, u32[]{:S(2)}) async-start(bf16[16,48,2048]{2,1,0:T(8,128)(2,1)} %get-tuple-element.14), calls=%async_computation | async-start | bytes 6291456 | tf_op jit(solution)/shard_map/all_to_all | solution.py:252
  247.8 3.1 fusion.7
  250.9 0.0 copy-done.2
  250.9 0.0 copy-start.6
  250.9 2.4 fusion.3
  253.4 3.0 psum.7
  256.4 0.0 copy-done.6
  256.4 9.9 %fusion = bf16[1,768,4096]{2,1,0:T(8,128)(2,1)} fusion(bf16[768,768]{1,0:T(8,128)(2,1)S(1)} %copy-done.6, bf16[768,4096]{1,0:T(8,128)(2,1)} %bitcast.57), kind=kOutput, calls=%fused_computation.4 | convolution fusion | flops 4834983936 | bytes 13762560 | tf_op jit(solution)/shard_map/dot_general | solution.py:291
  266.3 0.0 copy-done.5
  266.4 10.0 %fusion.1 = bf16[1,768,4096]{2,1,0:T(8,128)(2,1)} fusion(bf16[768,768]{1,0:T(8,128)(2,1)S(1)} %copy-done.5, bf16[768,4096]{1,0:T(8,128)(2,1)} %bitcast.58), kind=kOutput, calls=%fused_computation.5 | convolution fusion | flops 4834983936 | bytes 13762560 | tf_op jit(solution)/shard_map/dot_general | solution.py:294
  276.3 0.0 slice-done
  276.3 0.0 slice-done.1
  276.3 0.0 copy-done.4
  276.3 0.0 copy-start.1
  276.3 7.1 %fusion.2 = bf16[1,768,4096]{2,1,0:T(8,128)(2,1)} fusion(bf16[768,768]{1,0:T(8,128)(2,1)S(1)} %copy-done.4, bf16[768,4096]{1,0:T(8,128)(2,1)S(1)} %bitcast.56), kind=kOutput, calls=%fused_computation.6 | convolution fusion | flops 4834983936 | bytes 13762560 | tf_op jit(solution)/shard_map/dot_general | solution.py:297
  283.4 34.4 %all-to-all-done = bf16[16,48,2048]{2,1,0:T(8,128)(2,1)} async-done(((bf16[16,48,2048]{2,1,0:T(8,128)(2,1)}), bf16[16,48,2048]{2,1,0:T(8,128)(2,1)}, u32[]{:S(2)}, u32[]{:S(2)}) %all-to-all-start) | async-done | bytes 3145760 | tf_op jit(solution)/shard_map/all_to_all | solution.py:252
  317.8 3.9 %convolution_convert_fusion.4 = bf16[256,2048]{1,0:T(8,128)(2,1)} fusion(bf16[768,2048]{1,0:T(8,128)(2,1)} %bitcast.10, s32[256]{0:T(256)S(1)} %bitcast.39, s32[256]{0:T(256)S(1)} %bitcast.44), kind=kOutput, calls=%fused_computation.10 | convolution fusion | flops 807403520 | bytes 4196352 | tf_op jit(solution)/shard_map/dot_general | solution.py:312
  321.7 0.0 copy-done.1
  (11 shorter events, 0.0 us)
Async XLA Ops:
  0.6 3.0 copy-start
  3.6 3.0 copy-start.3
  239.8 78.0 %all-to-all-start = ((bf16[16,48,2048]{2,1,0:T(8,128)(2,1)}), bf16[16,48,2048]{2,1,0:T(8,128)(2,1)}, u32[]{:S(2)}, u32[]{:S(2)}) async-start(bf16[16,48,2048]{2,1,0:T(8,128)(2,1)} %get-tuple-element.14), calls=%async_computation | async-start | bytes 6291456 | tf_op jit(solution)/shard_map/all_to_all | solution.py:252
  247.8 3.1 copy-start.2
  250.9 5.5 %copy-start.6 = (bf16[768,768]{1,0:T(8,128)(2,1)S(1)}, bf16[768,768]{1,0:T(8,128)(2,1)}, u32[]{:S(2)}) copy-start(bf16[768,768]{1,0:T(8,128)(2,1)} %get-tuple-element.15) | copy-start | bytes 3538948
  256.4 10.0 %copy-start.5 = (bf16[768,768]{1,0:T(8,128)(2,1)S(1)}, bf16[768,768]{1,0:T(8,128)(2,1)}, u32[]{:S(2)}) copy-start(bf16[768,768]{1,0:T(8,128)(2,1)} %get-tuple-element.17) | copy-start | bytes 3538948
  256.4 19.9 %slice-start = ((s8[6291456]{0:T(1024)(128)(4,1)}), s8[4194304]{0:T(1024)(128)(4,1)S(1)}, s32[]{:S(2)}) async-start(s8[6291456]{0:T(1024)(128)(4,1)} %bitcast.54), calls=%async_computation.1 | async-start | bytes 8388608
  266.3 10.0 %slice-start.1 = ((s8[6291456]{0:T(1024)(128)(4,1)}), s8[2097152]{0:T(1024)(128)(4,1)S(1)}, s32[]{:S(2)}) async-start(s8[6291456]{0:T(1024)(128)(4,1)} %bitcast.54), calls=%async_computation.2 | async-start | bytes 4194304
  266.4 10.0 %copy-start.4 = (bf16[768,768]{1,0:T(8,128)(2,1)S(1)}, bf16[768,768]{1,0:T(8,128)(2,1)}, u32[]{:S(2)}) copy-start(bf16[768,768]{1,0:T(8,128)(2,1)} %get-tuple-element.18) | copy-start | bytes 3538948
  276.3 45.4 %copy-start.1 = (bf16[256,2048]{1,0:T(8,128)(2,1)S(1)}, bf16[256,2048]{1,0:T(8,128)(2,1)}, u32[]{:S(2)}) copy-start(bf16[256,2048]{1,0:T(8,128)(2,1)} %param.7) | copy-start | bytes 3145732

commit v4 on v3

--- a/solution.py
+++ b/solution.py
@@ -27,7 +27,7 @@
     cap, part = send_x.shape[1:]
     rows = n * cap
     units = wg.shape[0]
-    ahead = n // 8
+    ahead = n // 4
     mine = pl.ds(pl.multiple_of(side * part, part), part)
 
     def peer(step):
@@ -147,7 +147,7 @@
     swap_out.wait()
     add(out_own, mate_out)
 
-    @pl.loop(1, 1 + ahead)
+    @pl.loop(1, 1 + 2 * ahead)
     def _(step):
         o_copy(step).start()
 
@@ -156,9 +156,9 @@
         g_copy(step).wait()
         handed(full_g, step, gm_out, gm_in).start()
 
-        @pl.when(step + ahead < n)
+        @pl.when(step + 2 * ahead < n)
         def _():
-            o_copy(step + ahead).start()
+            o_copy(step + 2 * ahead).start()
 
     own_out = pltpu.make_async_copy(out_own.at[me], back_out.at[me], local_sem.at[5])
     own_out.start()

time: 322 us -> 319 us (level)
  Pallas kernels: 231 us -> 227 us
    pallas_call x1, Pallas kernels: 231 us -> 227 us  [run_middle(): pl.pallas_call(functools.partial(middle, n), out_shape=(full, full, acts,...]
where the time goes in v4:
time: 319 us; the launch traced here: 318 us
  Pallas kernels  227 us (71%)
  matrix products  42 us (13%)
  waiting for transfers between devices  34.6 us (11%)
  starting transfers between devices  7.88 us (2%)
    pallas_call x1, Pallas kernels, run_middle(): pl.pallas_call(functools.partial(middle, n), out_shape=(full, full, acts,...  227 us
    all_to_all x1, waiting for transfers between devices, exchange(): moved = lax.all_to_all(cut, 'dp', split_axis=0, concat_axis=0, tiled=True)  34.6 us
    dot_general x1, matrix products, shards(): lax.dot_general(dup, rows_x, outer, preferred_element_type=jnp.float32)  9.96 us
    dot_general x1, matrix products, shards(): lax.dot_general(dgate, rows_x, outer, preferred_element_type=jnp.float32)  9.95 us
    all_to_all x1, starting transfers between devices, exchange(): moved = lax.all_to_all(cut, 'dp', split_axis=0, concat_axis=0, tiled=True)  7.88 us
    dot_general x1, matrix products, shards(): lax.dot_general(hidden, rows_g, outer, preferred_element_type=jnp.float32)  7.08 us
  transfers between devices with their start and end apart: 1, of which 1 were waited for; matrix products, arithmetic and copies ran while one was open for 10% of the time, Pallas kernels for 0%

profile of v4, /device:TPU:12, one launch (start us, length us, event | category | flops | bytes accessed | tf_op | source)
XLA Modules:
  0.0 318.3 jit_solution(2652294852953873095)
XLA Ops:
  0.6 0.0 copy-start
  0.6 0.8 fusion.27
  1.4 0.8 copy.22
  2.3 0.1 eq.71
  2.4 0.3 fusion.5
  2.7 0.1 convert_element_type.48
  2.8 0.1 copy.23
  2.9 0.7 multiply_add_fusion
  3.6 0.0 copy-done
  3.6 2.7 convolution_convert_fusion.3
  6.3 0.3 select_reduce_fusion
  6.6 0.0 copy-done.3
  6.6 2.7 multiply_convert_fusion
  9.2 227.1 %shard_map.118 = (bf16[16,48,4096]{2,1,0:T(8,128)(2,1)}, bf16[16,48,4096]{2,1,0:T(8,128)(2,1)}, bf16[768,768]{1,0:T(8,128)(2,1)}, bf16[768,768]{1,0:T(8,128)(2,1...) custom-call(bf16[16,48,2048]{2,1,0:T(8,128)(2,1)} %bitcast.32, ...), custom_call_target="tpu_custom_call" | custom-call | flops 28991029248 | bytes 60000000 | tf_op jit(solution)/shard_map/pallas_call | solution.py:206
  236.4 7.9 %all-to-all-start = ((bf16[16,48,2048]{2,1,0:T(8,128)(2,1)}), bf16[16,48,2048]{2,1,0:T(8,128)(2,1)}, u32[]{:S(2)}, u32[]{:S(2)}) async-start(bf16[16,48,2048]{2,1,0:T(8,128)(2,1)} %get-tuple-element.14), calls=%async_computation | async-start | bytes 6291456 | tf_op jit(solution)/shard_map/all_to_all | solution.py:252
  244.3 3.1 fusion.7
  247.3 0.0 copy-done.2
  247.3 0.0 copy-start.6
  247.4 2.4 fusion.3
  249.8 3.0 psum.7
  252.8 0.0 copy-done.6
  252.8 9.9 %fusion = bf16[1,768,4096]{2,1,0:T(8,128)(2,1)} fusion(bf16[768,768]{1,0:T(8,128)(2,1)S(1)} %copy-done.6, bf16[768,4096]{1,0:T(8,128)(2,1)} %bitcast.57), kind=kOutput, calls=%fused_computation.4 | convolution fusion | flops 4834983936 | bytes 13762560 | tf_op jit(solution)/shard_map/dot_general | solution.py:291
  262.8 0.0 copy-done.5
  262.8 10.0 %fusion.1 = bf16[1,768,4096]{2,1,0:T(8,128)(2,1)} fusion(bf16[768,768]{1,0:T(8,128)(2,1)S(1)} %copy-done.5, bf16[768,4096]{1,0:T(8,128)(2,1)} %bitcast.58), kind=kOutput, calls=%fused_computation.5 | convolution fusion | flops 4834983936 | bytes 13762560 | tf_op jit(solution)/shard_map/dot_general | solution.py:294
  272.7 0.0 slice-done
  272.7 0.0 slice-done.1
  272.7 0.0 copy-done.4
  272.8 0.0 copy-start.1
  272.8 7.1 %fusion.2 = bf16[1,768,4096]{2,1,0:T(8,128)(2,1)} fusion(bf16[768,768]{1,0:T(8,128)(2,1)S(1)} %copy-done.4, bf16[768,4096]{1,0:T(8,128)(2,1)S(1)} %bitcast.56), kind=kOutput, calls=%fused_computation.6 | convolution fusion | flops 4834983936 | bytes 13762560 | tf_op jit(solution)/shard_map/dot_general | solution.py:297
  279.9 34.6 %all-to-all-done = bf16[16,48,2048]{2,1,0:T(8,128)(2,1)} async-done(((bf16[16,48,2048]{2,1,0:T(8,128)(2,1)}), bf16[16,48,2048]{2,1,0:T(8,128)(2,1)}, u32[]{:S(2)}, u32[]{:S(2)}) %all-to-all-start) | async-done | bytes 3145760 | tf_op jit(solution)/shard_map/all_to_all | solution.py:252
  314.4 3.9 %convolution_convert_fusion.4 = bf16[256,2048]{1,0:T(8,128)(2,1)} fusion(bf16[768,2048]{1,0:T(8,128)(2,1)} %bitcast.10, s32[256]{0:T(256)S(1)} %bitcast.39, s32[256]{0:T(256)S(1)} %bitcast.44), kind=kOutput, calls=%fused_computation.10 | convolution fusion | flops 807403520 | bytes 4196352 | tf_op jit(solution)/shard_map/dot_general | solution.py:312
  318.3 0.0 copy-done.1
  (11 shorter events, 0.0 us)
Async XLA Ops:
  0.6 3.0 copy-start
  3.6 3.0 copy-start.3
  236.4 78.0 %all-to-all-start = ((bf16[16,48,2048]{2,1,0:T(8,128)(2,1)}), bf16[16,48,2048]{2,1,0:T(8,128)(2,1)}, u32[]{:S(2)}, u32[]{:S(2)}) async-start(bf16[16,48,2048]{2,1,0:T(8,128)(2,1)} %get-tuple-element.14), calls=%async_computation | async-start | bytes 6291456 | tf_op jit(solution)/shard_map/all_to_all | solution.py:252
  244.3 3.1 copy-start.2
  247.3 5.5 %copy-start.6 = (bf16[768,768]{1,0:T(8,128)(2,1)S(1)}, bf16[768,768]{1,0:T(8,128)(2,1)}, u32[]{:S(2)}) copy-start(bf16[768,768]{1,0:T(8,128)(2,1)} %get-tuple-element.15) | copy-start | bytes 3538948
  252.8 10.0 %copy-start.5 = (bf16[768,768]{1,0:T(8,128)(2,1)S(1)}, bf16[768,768]{1,0:T(8,128)(2,1)}, u32[]{:S(2)}) copy-start(bf16[768,768]{1,0:T(8,128)(2,1)} %get-tuple-element.17) | copy-start | bytes 3538948
  252.8 19.9 %slice-start = ((s8[6291456]{0:T(1024)(128)(4,1)}), s8[4194304]{0:T(1024)(128)(4,1)S(1)}, s32[]{:S(2)}) async-start(s8[6291456]{0:T(1024)(128)(4,1)} %bitcast.54), calls=%async_computation.1 | async-start | bytes 8388608
  262.8 10.0 %slice-start.1 = ((s8[6291456]{0:T(1024)(128)(4,1)}), s8[2097152]{0:T(1024)(128)(4,1)S(1)}, s32[]{:S(2)}) async-start(s8[6291456]{0:T(1024)(128)(4,1)} %bitcast.54), calls=%async_computation.2 | async-start | bytes 4194304
  262.8 10.0 %copy-start.4 = (bf16[768,768]{1,0:T(8,128)(2,1)S(1)}, bf16[768,768]{1,0:T(8,128)(2,1)}, u32[]{:S(2)}) copy-start(bf16[768,768]{1,0:T(8,128)(2,1)} %get-tuple-element.18) | copy-start | bytes 3538948
  272.8 45.6 %copy-start.1 = (bf16[256,2048]{1,0:T(8,128)(2,1)S(1)}, bf16[256,2048]{1,0:T(8,128)(2,1)}, u32[]{:S(2)}) copy-start(bf16[256,2048]{1,0:T(8,128)(2,1)} %param.7) | copy-start | bytes 3145732
